TPU v7x, 32 devices: a whole 2x2x4 slice. The times are simulated.
32 devices in a mesh: groups: 2 (over y), ffn: 4 (over z), side: 2 (over x), head: 2 (over core).
Axes of the slice: x: 2, y: 2, z: 4, core: 2. Of those that a mesh axis runs over, the one named last changes fastest.
Arguments:
- resid: bfloat16 [64, 8192], P('groups', ('ffn', 'side')), parts along dimension 0, may hold values from -6 to 6
- queries: bfloat16 [80, 8192], P(('groups', 'ffn', 'side'), 'head'), parts along dimension 0, may hold values from -240 to 240
- cache_keys: bfloat16 [80, 128, 512], P(('groups', 'ffn', 'side'), None, 'head'), parts along dimension 0, may hold values from -6 to 6
- cache_values: bfloat16 [80, 128, 512], P(('groups', 'ffn', 'side'), None, 'head'), parts along dimension 0, may hold values from -6 to 6
- assign: int32 [64], P('groups'), parts along dimension 0, may hold values from 0 to 7, as said below
- lengths: int32 [64], P('groups'), parts along dimension 0, may hold values from 1 to 128, as said below
- out_weight: bfloat16 [8192, 8192], P('head', ('ffn', 'side')), may hold values from -0.0625 to 0.0625
- norm_gain: float32 [8192], replicated, may hold values from 0.1 to 1.9
- w_gate: bfloat16 [8192, 26624], P(None, ('ffn', 'side', 'head')), may hold values from -0.0625 to 0.0625
- w_up: bfloat16 [8192, 26624], P(None, ('ffn', 'side', 'head')), may hold values from -0.0625 to 0.0625
- w_down: bfloat16 [26624, 8192], P(('ffn', 'side', 'head')), may hold values from -0.0390625 to 0.0390625
Outputs:
- updated: bfloat16 [64, 8192], P(('groups', 'ffn', 'side', 'head')), parts along dimension 0
There are 2 independent parts, one for each index of `groups`. A program takes and returns all parts, laid end to end along the dimension named above; an argument that names none is the same for every part. Nothing has to cross between parts.
Inputs may be any that keep to these rules, and one draw needn't show every extreme that they name: `assign`: each attention device receives at most 5 rows, and some device exactly 5. `lengths`: some row has exactly 128.
All inputs are finite; a program needn't handle non-finite values.
Results may differ from a plain program's by a relative error of at most 0.0054.
Values may be sent and summed in bfloat16 or wider, within the bound.
A program may use at most 192 MiB of HBM per device.

v0:
```python
import jax
import jax.numpy as jnp
from jax import lax
from jax.sharding import PartitionSpec as P

D = 8192
HD = 128


def slot_numbers(assign, att_count, cap):
    owners = jnp.arange(att_count, dtype=jnp.int32)
    onehot = (assign[:, None] == owners[None, :]).astype(jnp.int32)
    before = jnp.cumsum(onehot, axis=0) - onehot
    rank = jnp.sum(before * onehot, axis=1)
    return assign * cap + rank


def shards(
    resid,
    queries,
    cache_keys,
    cache_values,
    assign,
    lengths,
    out_weight,
    norm_gain,
    w_gate,
    w_up,
    w_down,
):
    cap = queries.shape[0]
    ctx = cache_keys.shape[1]
    kv_local = cache_keys.shape[2] // HD
    q_local = queries.shape[1] // HD
    group = q_local // kv_local
    cols = resid.shape[1]
    att_count = lax.axis_size(("ffn", "side"))
    device = lax.axis_index(("ffn", "side"))
    slot_of = slot_numbers(assign, att_count, cap)
    wanted = device * cap + jnp.arange(cap, dtype=jnp.int32)
    match = slot_of[:, None] == wanted[None, :]
    slot_len = jnp.sum(jnp.where(match, lengths[:, None], 0), axis=0)
    qh = queries.reshape(cap, kv_local, group, HD)
    kh = cache_keys.reshape(cap, ctx, kv_local, HD)
    vh = cache_values.reshape(cap, ctx, kv_local, HD)
    scores = jnp.einsum("ckgd,ctkd->ckgt", qh, kh, preferred_element_type=jnp.float32) * (
        1.0 / float(HD) ** 0.5
    )
    mask = (jnp.arange(ctx, dtype=jnp.int32)[None, :] < slot_len[:, None])[:, None, None, :]
    top = jnp.max(jnp.where(mask, scores, -1e30), axis=-1, keepdims=True)
    weights = jnp.where(mask, jnp.exp(scores - top), 0.0)
    total = jnp.sum(weights, axis=-1, keepdims=True)
    total = jnp.where(slot_len[:, None, None, None] > 0, total, 1.0)
    probs = (weights / total).astype(jnp.bfloat16)
    attended = jnp.einsum("ckgt,ctkd->ckgd", probs, vh, preferred_element_type=jnp.float32)
    attended = attended.astype(jnp.bfloat16).reshape(cap, q_local * HD)
    partial_out = jnp.dot(
        lax.all_gather(attended, ("ffn", "side"), axis=0, tiled=True),
        out_weight,
        preferred_element_type=jnp.float32,
    )
    slot_out = lax.psum(partial_out, "head")
    mixed = resid.astype(jnp.float32) + jnp.take(slot_out, slot_of, axis=0)
    col_start = device * cols
    squares = jnp.sum(mixed * mixed, axis=1)
    meansq = lax.psum(squares, ("ffn", "side")) / D
    gain_local = lax.dynamic_slice_in_dim(norm_gain, col_start, cols, 0)
    normed = (mixed * lax.rsqrt(meansq + 1e-05)[:, None] * gain_local[None, :]).astype(jnp.bfloat16)
    piece = lax.all_gather(normed, ("ffn", "side"), axis=1, tiled=True)
    gate = jnp.dot(piece, w_gate, preferred_element_type=jnp.float32)
    up = jnp.dot(piece, w_up, preferred_element_type=jnp.float32)
    hidden = (jax.nn.silu(gate) * up).astype(jnp.bfloat16)
    product = jnp.dot(hidden, w_down, preferred_element_type=jnp.float32)
    carried = mixed * 0.5
    block = lax.dynamic_slice_in_dim(product, col_start, cols, 1) + carried
    summed = lax.psum_scatter(
        lax.dynamic_update_slice_in_dim(product, block, col_start, 1),
        ("ffn", "side", "head"),
        scatter_dimension=0,
        tiled=True,
    )
    return summed.astype(jnp.bfloat16)


def solution(mesh):
    in_specs = (
        P("groups", ("ffn", "side")),
        P(("groups", "ffn", "side"), "head"),
        P(("groups", "ffn", "side"), None, "head"),
        P(("groups", "ffn", "side"), None, "head"),
        P("groups"),
        P("groups"),
        P("head", ("ffn", "side")),
        P(),
        P(None, ("ffn", "side", "head")),
        P(None, ("ffn", "side", "head")),
        P(("ffn", "side", "head"), None),
    )
    out_specs = P(("groups", "ffn", "side", "head"), None)
    return jax.shard_map(shards, mesh=mesh, in_specs=in_specs, out_specs=out_specs, check_vma=False)
```

profile of v0, /device:TPU:0, one launch (start us, length us, event | category | flops | bytes accessed | tf_op | source)
XLA Modules:
  0.0 235.7 jit_solution(7477753203880768030)
XLA Ops:
  6.5 0.0 copy-start
  6.5 0.0 all-reduce.4.cloned.1.call-start
  6.5 0.8 fusion.20
  7.3 0.1 reduce_window_sum.11
  7.4 0.8 select_reduce_fusion.1
  8.2 0.7 compare_and_fusion
  8.9 0.8 select_reduce_fusion.2
  9.7 0.1 iota_compare_fusion.1
  9.8 0.8 copy.22
  10.6 0.0 copy-done
  10.7 0.3 convolution_multiply_fusion.1
  10.9 0.2 fusion.31
  11.1 0.1 broadcast_select_fusion
  11.2 1.3 convolution_convert_fusion
  12.5 0.1 reshape.67
  12.6 33.0 %all-gather = bf16[8,5,4096]{2,1,0:T(8,128)(2,1)S(1)} all-gather(bf16[1,5,4096]{2,1,0:T(8,128)(2,1)S(1)} %reshape.67), channel_id=1, replica_groups=mesh['groups'=2,'ffn'=4,'side'=2,'head'=2] {'ffn','side'}, dimensions={0}, use_global_device_ids=true | all-gather | bytes 368640 | tf_op jit(solution)/shard_map/all_gather | solution.py:58
  45.6 0.1 reshape.68
  45.8 5.6 %fusion.32 = f32[40,1024]{1,0:T(8,128)} fusion(bf16[40,4096]{1,0:T(8,128)(2,1)S(1)} %reshape.68, bf16[4096,1024]{1,0:T(8,128)(2,1)} %param.17), kind=kOutput, calls=%fused_computation.50 | convolution fusion | flops 335544320 | bytes 8880128 | tf_op jit(solution)/shard_map/dot_general | solution.py:57
  51.4 0.0 all-reduce.4.cloned.1.call-update
  51.4 0.7 dynamic_slice.6
  52.1 1.2 dynamic-slice
  54.0 16.7 %all-reduce.4.cloned.1.call-done = f32[40,1024]{1,0:T(8,128)} async-done(((f32[40,1024]{1,0:T(8,128)}), f32[40,1024]{1,0:T(8,128)}) %all-reduce.4.cloned.1.call-update) | async-done | bytes 163856 | tf_op jit(solution)/shard_map/psum | solution.py:62
  70.7 1.6 gather_fusion
  72.3 1.0 multiply_reduce_fusion
  73.3 21.6 %psum.15 = f32[32]{0:T(128)S(1)} all-reduce(f32[32]{0:T(128)S(1)} %multiply_reduce_fusion), channel_id=1, replica_groups=mesh['groups'=2,'ffn'=4,'side'=2,'head'=2] {'ffn','side'}, use_global_device_ids=true, to_apply=%region_7.8 | all-reduce | flops 32 | bytes 256 | tf_op jit(solution)/shard_map/psum | solution.py:66
  94.9 0.9 multiply_convert_fusion
  95.9 31.3 %all_gather.7 = bf16[32,8192]{1,0:T(8,128)(2,1)S(1)} all-gather(bf16[32,1024]{1,0:T(8,128)(2,1)S(1)} %multiply_convert_fusion), channel_id=1, replica_groups=mesh['groups'=2,'ffn'=4,'side'=2,'head'=2] {'ffn','side'}, dimensions={1}, use_global_device_ids=true | all-gather | bytes 589824 | tf_op jit(solution)/shard_map/all_gather | solution.py:69
  127.1 0.0 copy-start.1
  127.2 11.2 %fusion.33 = f32[32,1664]{1,0:T(8,128)S(1)} fusion(bf16[32,8192]{1,0:T(8,128)(2,1)S(1)} %all_gather.7, bf16[8192,1664]{1,0:T(8,128)(2,1)} %param.19), kind=kOutput, calls=%fused_computation.51 | convolution fusion | flops 872415232 | bytes 28000256 | tf_op jit(solution)/shard_map/dot_general | solution.py:70
  138.3 0.0 copy-start.2
  138.3 20.4 %fusion.2 = f32[32,8192]{1,0:T(8,128)S(1)} fusion(bf16[1664,8192]{1,0:T(8,128)(2,1)} %param.21, bf16[32,8192]{1,0:T(8,128)(2,1)S(1)} %all_gather.7, bf16[8192,1664]{1,0:T(8,128)(2,1)} %param.20, f32[32,1664]{1,0:T(8,128)S(1)} %fusion.33), kind=kOutput, calls=%fused_computation.4 | convolution fusion | flops 1745149952 | bytes 56311808 | tf_op jit(solution)/shard_map/dot_general | solution.py:73
  158.8 0.0 copy-done.2
  158.8 0.1 add_dynamic-update-slice_fusion
  158.9 69.3 %all-reduce.5 = bf16[32,8192]{1,0:T(8,128)(2,1)S(1)} all-reduce(f32[32,8192]{1,0:T(8,128)S(1)} %add_dynamic-update-slice_fusion), channel_id=2, replica_groups=mesh['groups'=2,'ffn'=4,'side'=2,'head'=2] {'ffn','side','head'}, use_global_device_ids=true, to_apply=%region_8.9.clone | all-reduce | flops 262144 | bytes 1572864
  228.2 0.7 dynamic-slice_convert_fusion
  228.9 0.0 copy-done.1
  (5 shorter events, 0.0 us)
Async XLA Ops:
  6.5 4.1 %copy-start = (bf16[5,128,256]{2,1,0:T(8,128)(2,1)S(1)}, bf16[5,128,256]{2,1,0:T(8,128)(2,1)}, u32[]{:S(2)}) copy-start(bf16[5,128,256]{2,1,0:T(8,128)(2,1)} %param.13) | copy-start | bytes 983044
  6.5 64.1 %all-reduce.4.cloned.1.call-start = ((), (), s32[]{:S(2)}) async-start(), calls=%async_computation | async-start | bytes 327680 | tf_op jit(solution)/shard_map/psum | solution.py:62
  127.1 101.8 %copy-start.1 = (bf16[5,128,256]{2,1,0:T(8,128)(2,1)S(1)}, bf16[5,128,256]{2,1,0:T(8,128)(2,1)}, u32[]{:S(2)}) copy-start(bf16[5,128,256]{2,1,0:T(8,128)(2,1)} %param.13) | copy-start | bytes 983044
  138.3 20.5 %copy-start.2 = (bf16[32,1024]{1,0:T(8,128)(2,1)S(1)}, bf16[32,1024]{1,0:T(8,128)(2,1)}, u32[]{:S(2)}) copy-start(bf16[32,1024]{1,0:T(8,128)(2,1)} %param.11) | copy-start | bytes 196612
Sparse Core Ops, SparseCore 0:
  51.5 19.1 all-reduce.3
where the time goes:
time: 236 us
  blocking collectives  155 us (66%)
  matrix products  38.8 us (16%)
  waiting for transfers between devices  16.7 us (7%)
  between operations  14.2 us (6%)
  other arithmetic  5.62 us (2%)
  local copies, waits for them, and re-layouts  5.25 us (2%)
    unnamed x1, blocking collectives  69.3 us
    all_gather x1, blocking collectives, shards(): lax.all_gather(attended, ('ffn', 'side'), axis=0, tiled=True)  33 us
    all_gather x1, blocking collectives, shards(): piece = lax.all_gather(normed, ('ffn', 'side'), axis=1, tiled=True)  31.3 us
    psum x1, blocking collectives, shards(): meansq = lax.psum(squares, ('ffn', 'side')) / D  21.6 us
    dot_general x1, matrix products, shards(): product = jnp.dot(hidden, w_down, preferred_element_type=jnp.float32)  20.4 us
    psum x1, waiting for transfers between devices, shards(): slot_out = lax.psum(partial_out, 'head')  16.7 us
    dot_general x1, matrix products, shards(): gate = jnp.dot(piece, w_gate, preferred_element_type=jnp.float32)  11.2 us
    dot_general x1, matrix products, shards(): jnp.dot(lax.all_gather(attended, ('ffn', 'side'), axis=0, tiled=True), ou...  5.59 us
  transfers between devices with their start and end apart: 1, of which 1 were waited for; matrix products, arithmetic and copies ran while one was open for 1% of the time, Pallas kernels for 0%

commit v1 on v0

--- a/solution.py
+++ b/solution.py
@@ -1,6 +1,10 @@
+import functools
+
 import jax
 import jax.numpy as jnp
 from jax import lax
+from jax.experimental import pallas as pl
+from jax.experimental.pallas import tpu as pltpu
 from jax.sharding import PartitionSpec as P
 
 D = 8192
@@ -82,6 +86,441 @@
     return summed.astype(jnp.bfloat16)
 
 
+NZ, NX, NH = 4, 2, 2
+GU_PAIRS = 11
+WD_SLOTS = 6
+EARLY = 3
+F32 = jnp.float32
+BF16 = jnp.bfloat16
+
+
+def iota(shape, dim):
+    return lax.broadcasted_iota(jnp.int32, shape, dim)
+
+
+def fused_kernel(
+    assign_ref, lengths_ref, gain_ref, resid_ref, q_ref, k_ref, v_ref,
+    wo_hbm, wg_hbm, wu_hbm, wd_hbm,
+    out_ref,
+    wo, gu, wd, qf, place, att, lhs, expart, exrecv, mixed, nrm, sq, acc, hidden,
+    prod, hrecv, s1, xsend, xrecv, s2, zf, zsend, zrecv, facc,
+    wo_sem, gu_sem, wd_sem, att_send, att_recv, ex_send, ex_recv, nrm_send, nrm_recv,
+    sq_send, sq_recv, h_send, h_recv, x_send, x_recv, z_send, z_recv,
+):
+    z, x, h = lax.axis_index("ffn"), lax.axis_index("side"), lax.axis_index("head")
+    dev = z * NX + x
+    own = dev * NH + h
+    other_x, other_h = 1 - x, 1 - h
+    rows, width = lhs.shape
+    half = nrm.shape[2]
+    slabs = nrm.shape[0]
+    cap = q_ref.shape[0]
+    group = qf.shape[0] // cap
+    kv = k_ref.shape[2] // HD
+
+    def z_at(step):
+        return lax.rem(z + step, NZ)
+
+    def to_z(step):
+        return {"ffn": z_at(step)}
+
+    to_x, to_h = {"side": other_x}, {"head": other_h}
+
+    def remote(src, dst, send, recv, where):
+        return pltpu.make_async_remote_copy(
+            src_ref=src, dst_ref=dst, send_sem=send, recv_sem=recv,
+            device_id=where, device_id_type=pl.DeviceIdType.MESH,
+        )
+
+    def slab_at(i):
+        zi = z_at(i)
+        xi = lax.rem(x + lax.div(i, NZ), NX)
+        hi = lax.rem(h + lax.div(i, NZ * NX), NH)
+        return (zi * NX + xi) * NH + hi
+
+    def wo_copy(j):
+        start = other_h if j == 0 else h
+        return pltpu.make_async_copy(
+            wo_hbm.at[:, pl.ds(pl.multiple_of(start * half, half), half)], wo.at[j], wo_sem.at[j]
+        )
+
+    def gu_copy(i, j):
+        slot = lax.rem(i, GU_PAIRS) * 2 + j
+        src = (wg_hbm, wu_hbm)[j]
+        start = pl.multiple_of(slab_at(i) * half, half)
+        return pltpu.make_async_copy(src.at[pl.ds(start, half), :], gu.at[slot], gu_sem.at[slot])
+
+    def wd_copy(c):
+        slot = lax.rem(c, WD_SLOTS)
+        start = pl.multiple_of(c * half, half)
+        return pltpu.make_async_copy(wd_hbm.at[:, pl.ds(start, half)], wd.at[slot], wd_sem.at[slot])
+
+    def start_pair(i, carry=0):
+        gu_copy(i, 0).start()
+        gu_copy(i, 1).start()
+        return carry
+
+    wo_copy(0).start()
+    wo_copy(1).start()
+    lax.fori_loop(0, EARLY, start_pair, 0)
+
+    barrier = pltpu.get_barrier_semaphore()
+    for where in (to_z(1), to_z(2), to_z(3), to_x, to_h):
+        pl.semaphore_signal(barrier, inc=1, device_id=where, device_id_type=pl.DeviceIdType.MESH)
+
+    a_row = jnp.broadcast_to(assign_ref[...].astype(F32), (rows, rows))
+    len_row = lengths_ref[...].astype(F32)
+    down, across = iota((rows, rows), 0), iota((rows, rows), 1)
+    a_col = jnp.sum(jnp.where(down == across, a_row, 0.0), axis=1, keepdims=True)
+    rank_row = jnp.sum(
+        jnp.where((a_col == a_row) & (down < across), 1.0, 0.0), axis=0, keepdims=True
+    )
+    slot_row = assign_ref[...].astype(F32) * cap + rank_row
+    cr = iota((group * cap, 1), 0)
+    of_slot = cr - cap * ((cr * 205) >> 10)
+    wanted = (dev * cap + of_slot).astype(F32)
+    slot_len = jnp.sum(
+        jnp.where(jnp.broadcast_to(slot_row, (group * cap, rows)) == wanted, len_row, 0.0),
+        axis=1, keepdims=True,
+    )
+    ctx = k_ref.shape[1]
+    mask = iota((group * cap, ctx), 1).astype(F32) < slot_len
+    for k in range(kv):
+        for g in range(group):
+            at = (k * group + g) * HD
+            qf[g * cap:(g + 1) * cap, :] = q_ref[:, at:at + HD].astype(F32)
+        qk = qf[...].astype(BF16)
+        keys = k_ref[:, :, k * HD:(k + 1) * HD].reshape(cap * ctx, HD)
+        values = v_ref[:, :, k * HD:(k + 1) * HD].reshape(cap * ctx, HD)
+        wide = lax.dot_general(qk, keys, (((1,), (1,)), ((), ())), preferred_element_type=F32)
+        scores = jnp.zeros((group * cap, ctx), F32)
+        for c in range(cap):
+            scores = jnp.where(of_slot == c, wide[:, c * ctx:(c + 1) * ctx], scores)
+        scores = scores * (1.0 / float(HD) ** 0.5)
+        top = jnp.max(jnp.where(mask, scores, -1e30), axis=-1, keepdims=True)
+        weights = jnp.where(mask, jnp.exp(scores - top), 0.0)
+        total = jnp.sum(weights, axis=-1, keepdims=True)
+        total = jnp.where(slot_len > 0.0, total, 1.0)
+        probs = weights / total
+        spread = jnp.concatenate(
+            [jnp.where(of_slot == c, probs, 0.0) for c in range(cap)], axis=1
+        ).astype(BF16)
+        att[dev, k] = jnp.dot(spread, values, preferred_element_type=F32).astype(BF16)
+
+    pl.semaphore_wait(barrier, 5)
+
+    def att_copy(d, sem, where):
+        return remote(att.at[d], att.at[d], att_send.at[sem], att_recv.at[d], where)
+
+    att_out = [att_copy(dev, t - 1, to_z(t)) for t in range(1, NZ)]
+    att_out.append(att_copy(dev, NZ - 1, to_x))
+    for copy in att_out:
+        copy.start()
+
+    lax.fori_loop(EARLY, GU_PAIRS, start_pair, 0)
+
+    def start_wd(c, carry):
+        wd_copy(c).start()
+        return carry
+
+    lax.fori_loop(0, WD_SLOTS, start_wd, 0)
+
+    pos = iota((rows, 1), 0)
+    each = rows // (NZ * NX * NH)
+    row_of = ((pos // each) % NZ) * (NX * NH * each) + ((pos // (each * NZ)) % NX) * (NH * each)
+    row_of = row_of + (pos // (each * NZ * NX)) * each + pos % each
+    row_pick = across == row_of
+    a_pos = jnp.sum(jnp.where(row_pick, a_row, 0.0), axis=1, keepdims=True)
+    rank_pos = jnp.sum(
+        jnp.where(row_pick, jnp.broadcast_to(rank_row, (rows, rows)), 0.0), axis=1, keepdims=True
+    )
+    target = a_pos * (group * cap) + rank_pos
+    lane = iota((rows, NZ * NX * group * cap), 1).astype(F32)
+    for g in range(group):
+        place[g * rows:(g + 1) * rows, :] = jnp.where(lane == target + g * cap, 1.0, 0.0).astype(BF16)
+    resid_half = resid_ref[:, pl.ds(pl.multiple_of(h * half, half), half)]
+    mixed[...] = jnp.dot(row_pick.astype(F32).astype(BF16), resid_half, preferred_element_type=F32)
+
+    for t in range(1, NZ):
+        d = z_at(t) * NX + x
+        att_copy(d, 0, to_x).wait_recv()
+        fwd = att_copy(d, NZ - 1 + t, to_x)
+        fwd.start()
+        att_out.append(fwd)
+    for t in range(NZ):
+        d = z_at(t) * NX + other_x
+        att_copy(d, 0, to_x).wait_recv()
+    for k in range(kv):
+        blocks = att[:, k].reshape(NZ * NX * group * cap, HD)
+        moved = jnp.dot(place[...], blocks, preferred_element_type=F32).astype(BF16)
+        for g in range(group):
+            at = (k * group + g) * HD
+            lhs[:, at:at + HD] = moved[g * rows:(g + 1) * rows, :]
+    for copy in att_out:
+        copy.wait_send()
+
+    depth = 512
+
+    def project(j):
+        def part(i, total):
+            start = pl.multiple_of(i * depth, depth)
+            return total + jnp.dot(
+                lhs[:, pl.ds(start, depth)], wo[j, pl.ds(start, depth), :],
+                preferred_element_type=F32,
+            )
+
+        return lax.fori_loop(0, width // depth, part, jnp.zeros((rows, half), F32))
+
+    wo_copy(0).wait()
+    expart[...] = project(0)
+    exchange = remote(expart, exrecv, ex_send, ex_recv, to_h)
+    exchange.start()
+    wo_copy(1).wait()
+    mixed[...] = mixed[...] + project(1)
+    exchange.wait()
+    mix = mixed[...] + exrecv[...]
+    mixed[...] = mix
+    gains = gain_ref[0:1, pl.ds(pl.multiple_of(own * half, half), half)]
+    nrm[own] = (mix * gains).astype(BF16)
+
+    def nrm_copy(s, sem, where):
+        return remote(nrm.at[s], nrm.at[s], nrm_send.at[sem], nrm_recv.at[s], where)
+
+    for t in range(1, NZ):
+        nrm_copy(own, t - 1, to_z(t)).start()
+    nrm_copy(own, NZ - 1, to_x).start()
+    nrm_copy(own, NZ, to_h).start()
+
+    squares = jnp.sum(mix * mix, axis=1, keepdims=True)
+    eye = iota((rows, HD), 0) == iota((rows, HD), 1)
+    squares_row = jnp.sum(jnp.where(eye, squares, 0.0), axis=0, keepdims=True)
+    sq[0] = jnp.broadcast_to(squares_row, (8, HD))
+
+    def sq_copy(t):
+        src, where = (0, to_z(t)) if t < NZ else ((NZ, to_x) if t == NZ else (NZ + 2, to_h))
+        dst = t if t < NZ else (NZ + 1 if t == NZ else NZ + 3)
+        return remote(sq.at[src], sq.at[dst], sq_send.at[t - 1], sq_recv.at[t - 1], where)
+
+    for t in range(1, NZ):
+        sq_copy(t).start()
+
+    acc[...] = jnp.zeros_like(acc)
+
+    def gate_up(i, carry):
+        s = slab_at(i)
+
+        @pl.when(i > 0)
+        def _():
+            nrm_copy(s, 0, to_h).wait_recv()
+
+        @pl.when((i > 0) & (i < NZ))
+        def _():
+            nrm_copy(s, NZ + i, to_x).start()
+
+        @pl.when((i > 0) & (i < NZ * NX))
+        def _():
+            nrm_copy(s, 2 * NZ - 1 + i, to_h).start()
+
+        @pl.when(i == NZ * NX)
+        def _():
+            for t in range(1, NZ):
+                sq_copy(t).wait()
+            sq[NZ] = sq[0] + sq[1] + sq[2] + sq[3]
+            sq_copy(NZ).start()
+
+        @pl.when(i == NZ * NX + NZ)
+        def _():
+            sq_copy(NZ).wait()
+            sq[NZ + 2] = sq[NZ] + sq[NZ + 1]
+            sq_copy(NZ + 1).start()
+
+        slot = lax.rem(i, GU_PAIRS) * 2
+        block = nrm[s]
+        gu_copy(i, 0).wait()
+        acc[0] += jnp.dot(block, gu[slot], preferred_element_type=F32)
+        gu_copy(i, 1).wait()
+        acc[1] += jnp.dot(block, gu[slot + 1], preferred_element_type=F32)
+
+        @pl.when(i + GU_PAIRS < slabs)
+        def _():
+            start_pair(i + GU_PAIRS)
+
+        return carry
+
+    lax.fori_loop(0, slabs, gate_up, 0)
+    sq_copy(NZ + 1).wait()
+    total_row = jnp.broadcast_to((sq[NZ + 2] + sq[NZ + 3])[0:1], (rows, HD))
+    total = jnp.sum(jnp.where(eye, total_row, 0.0), axis=1, keepdims=True)
+    scale = lax.rsqrt(total / D + 1e-05)
+    gate = acc[0] * scale
+    up = acc[1] * scale
+    hidden[...] = (gate / (1.0 + jnp.exp(-gate)) * up).astype(BF16)
+
+    batches = prod.shape[0]
+    per = slabs // batches
+    span = prod.shape[2]
+    seg = zf.shape[3]
+    hrows = rows // NH
+    xrows = hrows // NX
+
+    def multiply(b):
+        def chunk(j, carry):
+            c = b * per + j
+            wd_copy(c).wait()
+            term = jnp.dot(hidden[...], wd[lax.rem(c, WD_SLOTS)], preferred_element_type=F32)
+            term = term + jnp.where(c == own, 1.0, 0.0) * mixed[...]
+            prod[b, :, pl.ds(pl.multiple_of(j * half, half), half)] = term
+
+            @pl.when(c + WD_SLOTS < slabs)
+            def _():
+                wd_copy(c + WD_SLOTS).start()
+
+            return carry
+
+        lax.fori_loop(0, per, chunk, 0)
+
+    def h_copy(b):
+        src = prod.at[b, pl.ds(pl.multiple_of(other_h * hrows, hrows), hrows), :]
+        return remote(src, hrecv.at[b], h_send.at[b], h_recv.at[b], to_h)
+
+    def x_copy(b):
+        return remote(xsend.at[b], xrecv.at[b], x_send.at[b], x_recv.at[b], to_x)
+
+    def z_copy(b, t):
+        sem = b * (NZ - 1) + t - 1
+        return remote(zsend.at[b, z_at(t)], zrecv.at[b, t - 1], z_send.at[sem], z_recv.at[sem], to_z(t))
+
+    def stage_x(b):
+        h_copy(b).wait()
+        s1[b] = prod[b, pl.ds(pl.multiple_of(h * hrows, hrows), hrows), :] + hrecv[b]
+        there = s1[b, pl.ds(pl.multiple_of(other_x * xrows, xrows), xrows), :]
+        xsend[b] = jnp.concatenate([there[:, :span // 2], there[:, span // 2:]], axis=0).astype(BF16)
+        x_copy(b).start()
+
+    def stage_z(b):
+        x_copy(b).wait()
+        here = s1[b, pl.ds(pl.multiple_of(x * xrows, xrows), xrows), :]
+        came = xrecv[b].astype(F32)
+        s2[b] = here + jnp.concatenate([came[:xrows], came[xrows:]], axis=1)
+        for q in range(NZ):
+            for m in range(span // seg):
+                zf[b, q, m * each:(m + 1) * each, :] = s2[b, q * each:(q + 1) * each, m * seg:(m + 1) * seg]
+        zsend[b] = zf[b].astype(BF16)
+        for t in range(1, NZ):
+            z_copy(b, t).start()
+
+    def stage_out(b):
+        for t in range(1, NZ):
+            z_copy(b, t).wait()
+        total = zf[b, z]
+        for t in range(1, NZ):
+            total = total + zrecv[b, t - 1].astype(F32)
+        facc[b] = total
+        for m in range(span // seg):
+            at = b * span + m * seg
+            out_ref[:, at:at + seg] = facc[b, m * each:(m + 1) * each, :].astype(BF16)
+
+    for step in range(batches + 3):
+        if step < batches:
+            multiply(step)
+            h_copy(step).start()
+        if 0 <= step - 1 < batches:
+            stage_x(step - 1)
+        if 0 <= step - 2 < batches:
+            stage_z(step - 2)
+        if 0 <= step - 3 < batches:
+            stage_out(step - 3)
+
+    for t in range(1, NZ):
+        nrm_copy(own, t - 1, to_z(t)).wait_send()
+    nrm_copy(own, NZ - 1, to_x).wait_send()
+    nrm_copy(own, NZ, to_h).wait_send()
+    for i in range(1, NZ):
+        nrm_copy(own, NZ + i, to_x).wait_send()
+    for i in range(1, NZ * NX):
+        nrm_copy(own, 2 * NZ - 1 + i, to_h).wait_send()
+
+
+def fused(
+    resid, queries, cache_keys, cache_values, assign, lengths,
+    out_weight, norm_gain, w_gate, w_up, w_down,
+):
+    rows, cols = resid.shape
+    cap = queries.shape[0]
+    ff = w_gate.shape[1]
+    half = cols // NH
+    slabs = NZ * NX * NH
+    kv = cache_keys.shape[2] // HD
+    group = queries.shape[1] // HD // kv
+    batches = 4
+    span = slabs * half // batches
+    each = rows // slabs
+    seg = span * each // 16
+    vmem = pl.BlockSpec(memory_space=pltpu.VMEM)
+    hbm = pl.BlockSpec(memory_space=pl.ANY)
+    dma = pltpu.SemaphoreType.DMA
+    V = pltpu.VMEM
+    weights = (out_weight.size + 3 * w_gate.size)
+    return pl.pallas_call(
+        fused_kernel,
+        out_shape=jax.ShapeDtypeStruct((each, slabs * half), BF16),
+        in_specs=[vmem] * 7 + [hbm] * 4,
+        out_specs=vmem,
+        scratch_shapes=[
+            V((NH, out_weight.shape[0], half), BF16),
+            V((2 * GU_PAIRS, half, ff), BF16),
+            V((WD_SLOTS, ff, half), BF16),
+            V((group * cap, HD), F32),
+            V((group * rows, NZ * NX * group * cap), BF16),
+            V((NZ * NX, kv, group * cap, HD), BF16),
+            V((rows, out_weight.shape[0]), BF16),
+            V((rows, half), F32),
+            V((rows, half), F32),
+            V((rows, half), F32),
+            V((slabs, rows, half), BF16),
+            V((NZ + 4, 8, HD), F32),
+            V((2, rows, ff), F32),
+            V((rows, ff), BF16),
+            V((batches, rows, span), F32),
+            V((batches, rows // NH, span), F32),
+            V((batches, rows // NH, span), F32),
+            V((batches, 16, span // 2), BF16),
+            V((batches, 16, span // 2), BF16),
+            V((batches, 8, span), F32),
+            V((batches, NZ, 16, seg), F32),
+            V((batches, NZ, 16, seg), BF16),
+            V((batches, NZ - 1, 16, seg), BF16),
+            V((batches, 16, seg), F32),
+            dma((NH,)),
+            dma((2 * GU_PAIRS,)),
+            dma((WD_SLOTS,)),
+            dma((2 * NZ,)),
+            dma((NZ * NX,)),
+            dma(()),
+            dma(()),
+            dma((2 * NZ + NZ * NX,)),
+            dma((slabs,)),
+            dma((NZ + 1,)),
+            dma((NZ + 1,)),
+            dma((batches,)),
+            dma((batches,)),
+            dma((batches,)),
+            dma((batches,)),
+            dma((batches * (NZ - 1),)),
+            dma((batches * (NZ - 1),)),
+        ],
+        cost_estimate=pl.CostEstimate(
+            flops=2 * rows * weights, bytes_accessed=2 * weights, transcendentals=rows * ff
+        ),
+        compiler_params=pltpu.CompilerParams(
+            collective_id=0, has_side_effects=True, vmem_limit_bytes=63 * 1024 * 1024
+        ),
+    )(
+        assign.reshape(1, rows), lengths.reshape(1, rows), norm_gain.reshape(1, -1),
+        resid, queries, cache_keys, cache_values, out_weight, w_gate, w_up, w_down,
+    )
+
+
 def solution(mesh):
     in_specs = (
         P("groups", ("ffn", "side")),
@@ -97,4 +536,6 @@
         P(("ffn", "side", "head"), None),
     )
     out_specs = P(("groups", "ffn", "side", "head"), None)
-    return jax.shard_map(shards, mesh=mesh, in_specs=in_specs, out_specs=out_specs, check_vma=False)
+    sizes = (mesh.shape["ffn"], mesh.shape["side"], mesh.shape["head"])
+    body = fused if sizes == (NZ, NX, NH) else shards
+    return jax.shard_map(body, mesh=mesh, in_specs=in_specs, out_specs=out_specs, check_vma=False)

time: 236 us -> 54.8 us (0.23)
  blocking collectives: 155 us -> 0 us
  Pallas kernels: 0 us -> 53.2 us
  matrix products: 38.8 us -> 0 us
  waiting for transfers between devices: 16.7 us -> 0 us
  between operations: 14.2 us -> 0.01 us
  other arithmetic: 5.62 us -> 0 us
  local copies, waits for them, and re-layouts: 5.25 us -> 1.4 us
    unnamed x1 -> x0, blocking collectives: 69.3 us -> none
    all_gather x2 -> x0, blocking collectives: 64.3 us -> none  [the longest x1 33 us: shards(): lax.all_gather(attended, ('ffn', 'side'), axis=0, tiled=True)]
    pallas_call x0 -> x1, Pallas kernels: none -> 53.2 us  [fused(): pl.pallas_call(fused_kernel, out_shape=jax.ShapeDtypeStruct((each, slabs...]
    dot_general x5 -> x0, matrix products: 38.8 us -> none  [the longest x1 20.4 us: shards(): product = jnp.dot(hidden, w_down, preferred_element_type=jnp.float32)]
    psum x1 -> x0, blocking collectives: 21.6 us -> none  [shards(): meansq = lax.psum(squares, ('ffn', 'side')) / D]
    psum x1 -> x0, waiting for transfers between devices: 16.7 us -> none  [shards(): slot_out = lax.psum(partial_out, 'head')]
    reduce_sum x3 -> x0, other arithmetic: 2.71 us -> none  [the longest x1 1.04 us: shards(): squares = jnp.sum(mixed * mixed, axis=1)]
  transfers between devices with their start and end apart: 1 -> 0, of which waited for: 1 -> 0; matrix products, arithmetic and copies ran while one was open for 1% -> 0% of each run, Pallas kernels for 0% -> 0%
where the time goes in v1:
time: 54.8 us; the launch traced here: 54.6 us
  Pallas kernels  53.2 us (97%)
  local copies, waits for them, and re-layouts  1.4 us (3%)
    pallas_call x1, Pallas kernels, fused(): pl.pallas_call(fused_kernel, out_shape=jax.ShapeDtypeStruct((each, slabs...  53.2 us
    unnamed x1, local copies, waits for them, and re-layouts  1.4 us

profile of v1, /device:TPU:0, one launch (start us, length us, event | category | flops | bytes accessed | tf_op | source)
XLA Modules:
  0.0 54.6 jit_solution(11333785765194503489)
XLA Ops:
  0.0 53.2 %shard_map.109 = bf16[2,8192]{1,0:T(2,128)(2,1)} custom-call(s32[1,32]{1,0:T(1,128)} %bitcast.4, s32[1,32]{1,0:T(1,128)} %bitcast.5, f32[1,8192]{1,0:T(1,128)} %bitcast.3, bf16[32,1024]{1,0:T(8,128)(2,1)} %resid_ref.1, bf16[5,4096]{1,0:T(8,128)(2,1)} %q_ref.1, bf16[5,128,256]{2,1,0:T(8,128)(2,1)} %k_ref.1, bf16[5,128,256]{2,1,0:T(8,128)(2,1)} %v_ref.1, ...), custom_call_target="tpu_custom_call" | custom-call | flops 2885681152 | bytes 90177536 | tf_op jit(solution)/shard_map/pallas_call | solution.py:464
  53.2 1.4 %copy.13 = bf16[2,8192]{1,0:T(2,128)(2,1)} copy(bf16[2,8192]{1,0:T(2,128)(2,1)} %shard_map.109) | data formatting | bytes 65536

commit v2 on v1

--- a/solution.py
+++ b/solution.py
@@ -87,9 +87,15 @@
 
 
 NZ, NX, NH = 4, 2, 2
-GU_PAIRS = 11
-WD_SLOTS = 6
-EARLY = 3
+PAIRS = 11
+WD_SLOTS = 3
+WO_PAIRS = 4
+EARLY = 2
+RUNS = ((0,), (1, 2), (3, 4, 5), (6,), (7, 8, 9, 10), (11, 12, 13), (14, 15))
+STEPS = (
+    (0, 0, 0), (0, 0, 1), (0, 1, 0), (1, 0, 0), (2, 0, 0), (3, 0, 0), (0, 1, 1), (1, 1, 0),
+    (2, 1, 0), (3, 1, 0), (1, 0, 1), (2, 0, 1), (3, 0, 1), (1, 1, 1), (2, 1, 1), (3, 1, 1),
+)
 F32 = jnp.float32
 BF16 = jnp.bfloat16
 
@@ -102,10 +108,10 @@
     assign_ref, lengths_ref, gain_ref, resid_ref, q_ref, k_ref, v_ref,
     wo_hbm, wg_hbm, wu_hbm, wd_hbm,
     out_ref,
-    wo, gu, wd, qf, place, att, lhs, expart, exrecv, mixed, nrm, sq, acc, hidden,
-    prod, hrecv, s1, xsend, xrecv, s2, zf, zsend, zrecv, facc,
+    gu, wd, qf, place, att, lhs, expart, exrecv, mixed, nrm, sq, acc, hidden,
+    prod, hrecv, s1, zf, zsend, zrecv, facc,
     wo_sem, gu_sem, wd_sem, att_send, att_recv, ex_send, ex_recv, nrm_send, nrm_recv,
-    sq_send, sq_recv, h_send, h_recv, x_send, x_recv, z_send, z_recv,
+    sq_send, sq_recv, h_send, h_recv, z_send, z_recv,
 ):
     z, x, h = lax.axis_index("ffn"), lax.axis_index("side"), lax.axis_index("head")
     dev = z * NX + x
@@ -119,7 +125,8 @@
     kv = k_ref.shape[2] // HD
 
     def z_at(step):
-        return lax.rem(z + step, NZ)
+        high = lax.rem(lax.div(z, 2) + step // 2, 2)
+        return high * 2 + lax.rem(z + step, 2)
 
     def to_z(step):
         return {"ffn": z_at(step)}
@@ -132,41 +139,43 @@
             device_id=where, device_id_type=pl.DeviceIdType.MESH,
         )
 
+    def chip(p):
+        return z_at(p // 2), lax.rem(x + p, NX)
+
     def slab_at(i):
-        zi = z_at(i)
-        xi = lax.rem(x + lax.div(i, NZ), NX)
-        hi = lax.rem(h + lax.div(i, NZ * NX), NH)
-        return (zi * NX + xi) * NH + hi
-
-    def wo_copy(j):
-        start = other_h if j == 0 else h
-        return pltpu.make_async_copy(
-            wo_hbm.at[:, pl.ds(pl.multiple_of(start * half, half), half)], wo.at[j], wo_sem.at[j]
-        )
+        dz, dx, dh = STEPS[i]
+        return (z_at(dz) * NX + lax.rem(x + dx, NX)) * NH + lax.rem(h + dh, NH)
+
+    def wo_copy(m):
+        src = wo_hbm.at[pl.ds(m * half, half), :]
+        dst = gu.at[m // WO_PAIRS, m % WO_PAIRS, :, pl.ds(0, wo_hbm.shape[1])]
+        return pltpu.make_async_copy(src, dst, wo_sem.at[m])
 
     def gu_copy(i, j):
-        slot = lax.rem(i, GU_PAIRS) * 2 + j
+        slot = (i + WO_PAIRS) % PAIRS
         src = (wg_hbm, wu_hbm)[j]
         start = pl.multiple_of(slab_at(i) * half, half)
-        return pltpu.make_async_copy(src.at[pl.ds(start, half), :], gu.at[slot], gu_sem.at[slot])
-
-    def wd_copy(c):
-        slot = lax.rem(c, WD_SLOTS)
-        start = pl.multiple_of(c * half, half)
-        return pltpu.make_async_copy(wd_hbm.at[:, pl.ds(start, half)], wd.at[slot], wd_sem.at[slot])
-
-    def start_pair(i, carry=0):
+        return pltpu.make_async_copy(src.at[pl.ds(start, half), :], gu.at[j, slot], gu_sem.at[j, slot])
+
+    def wd_copy(b):
+        slot = b % WD_SLOTS
+        span = wd.shape[2]
+        return pltpu.make_async_copy(wd_hbm.at[:, pl.ds(b * span, span)], wd.at[slot], wd_sem.at[slot])
+
+    def start_pair(i):
         gu_copy(i, 0).start()
         gu_copy(i, 1).start()
-        return carry
-
-    wo_copy(0).start()
-    wo_copy(1).start()
-    lax.fori_loop(0, EARLY, start_pair, 0)
 
     barrier = pltpu.get_barrier_semaphore()
-    for where in (to_z(1), to_z(2), to_z(3), to_x, to_h):
+    for p in range(1, NZ * NX):
+        zi, xi = chip(p)
+        where = {"ffn": zi, "side": xi}
         pl.semaphore_signal(barrier, inc=1, device_id=where, device_id_type=pl.DeviceIdType.MESH)
+    pl.semaphore_signal(barrier, inc=1, device_id=to_h, device_id_type=pl.DeviceIdType.MESH)
+    for m in range(2 * WO_PAIRS):
+        wo_copy(m).start()
+    for i in range(EARLY):
+        start_pair(i)
 
     a_row = jnp.broadcast_to(assign_ref[...].astype(F32), (rows, rows))
     len_row = lengths_ref[...].astype(F32)
@@ -207,7 +216,7 @@
         ).astype(BF16)
         att[dev, k] = jnp.dot(spread, values, preferred_element_type=F32).astype(BF16)
 
-    pl.semaphore_wait(barrier, 5)
+    pl.semaphore_wait(barrier, NZ * NX)
 
     def att_copy(d, sem, where):
         return remote(att.at[d], att.at[d], att_send.at[sem], att_recv.at[d], where)
@@ -217,13 +226,10 @@
     for copy in att_out:
         copy.start()
 
-    lax.fori_loop(EARLY, GU_PAIRS, start_pair, 0)
-
-    def start_wd(c, carry):
-        wd_copy(c).start()
-        return carry
-
-    lax.fori_loop(0, WD_SLOTS, start_wd, 0)
+    for i in range(EARLY, PAIRS - WO_PAIRS):
+        start_pair(i)
+    for b in range(WD_SLOTS):
+        wd_copy(b).start()
 
     pos = iota((rows, 1), 0)
     each = rows // (NZ * NX * NH)
@@ -259,24 +265,27 @@
     for copy in att_out:
         copy.wait_send()
 
-    depth = 512
-
-    def project(j):
-        def part(i, total):
-            start = pl.multiple_of(i * depth, depth)
-            return total + jnp.dot(
-                lhs[:, pl.ds(start, depth)], wo[j, pl.ds(start, depth), :],
+    def project(start):
+        cols = pl.ds(pl.multiple_of(start * half, half), half)
+        total = None
+        for j in range(2):
+            depth = WO_PAIRS * half
+            term = jnp.dot(
+                lhs[:, j * depth:(j + 1) * depth],
+                gu[j, 0:WO_PAIRS, :, cols].reshape(depth, half),
                 preferred_element_type=F32,
             )
-
-        return lax.fori_loop(0, width // depth, part, jnp.zeros((rows, half), F32))
-
-    wo_copy(0).wait()
-    expart[...] = project(0)
+            total = term if total is None else total + term
+        return total
+
+    for m in range(2 * WO_PAIRS):
+        wo_copy(m).wait()
+    expart[...] = project(other_h)
     exchange = remote(expart, exrecv, ex_send, ex_recv, to_h)
     exchange.start()
-    wo_copy(1).wait()
-    mixed[...] = mixed[...] + project(1)
+    mixed[...] = mixed[...] + project(h)
+    for i in range(PAIRS - WO_PAIRS, PAIRS):
+        start_pair(i)
     exchange.wait()
     mix = mixed[...] + exrecv[...]
     mixed[...] = mix
@@ -304,50 +313,57 @@
     for t in range(1, NZ):
         sq_copy(t).start()
 
-    acc[...] = jnp.zeros_like(acc)
-
-    def gate_up(i, carry):
-        s = slab_at(i)
-
-        @pl.when(i > 0)
-        def _():
-            nrm_copy(s, 0, to_h).wait_recv()
-
-        @pl.when((i > 0) & (i < NZ))
-        def _():
-            nrm_copy(s, NZ + i, to_x).start()
-
-        @pl.when((i > 0) & (i < NZ * NX))
-        def _():
-            nrm_copy(s, 2 * NZ - 1 + i, to_h).start()
-
-        @pl.when(i == NZ * NX)
-        def _():
+    def arrived(i):
+        nrm_copy(slab_at(i), 0, to_h).wait_recv()
+
+    def pass_on(i, sem, where):
+        nrm_copy(slab_at(i), sem, where).start()
+
+    loaded = PAIRS
+    for run in RUNS:
+        first, count = run[0], len(run)
+        if first == 1:
+            arrived(2)
+            pass_on(2, NZ + 1, to_h)
+            arrived(1)
+        elif first == 3:
+            for i in run:
+                arrived(i)
+                pass_on(i, NZ - 1 + i, to_x)
+                pass_on(i, 2 * NZ - 2 + i, to_h)
+        elif first == 7:
+            for i in run[:-1]:
+                arrived(i)
+                pass_on(i, 2 * NZ - 3 + i, to_h)
+            arrived(run[-1])
             for t in range(1, NZ):
                 sq_copy(t).wait()
             sq[NZ] = sq[0] + sq[1] + sq[2] + sq[3]
             sq_copy(NZ).start()
-
-        @pl.when(i == NZ * NX + NZ)
-        def _():
+        elif first > 0:
+            for i in run:
+                arrived(i)
+        if first == 11:
             sq_copy(NZ).wait()
             sq[NZ + 2] = sq[NZ] + sq[NZ + 1]
             sq_copy(NZ + 1).start()
-
-        slot = lax.rem(i, GU_PAIRS) * 2
-        block = nrm[s]
-        gu_copy(i, 0).wait()
-        acc[0] += jnp.dot(block, gu[slot], preferred_element_type=F32)
-        gu_copy(i, 1).wait()
-        acc[1] += jnp.dot(block, gu[slot + 1], preferred_element_type=F32)
-
-        @pl.when(i + GU_PAIRS < slabs)
-        def _():
-            start_pair(i + GU_PAIRS)
-
-        return carry
-
-    lax.fori_loop(0, slabs, gate_up, 0)
+        for i in run:
+            gu_copy(i, 0).wait()
+            gu_copy(i, 1).wait()
+        slot = (first + WO_PAIRS) % PAIRS
+        block = jnp.concatenate([nrm[slab_at(i)] for i in run], axis=1)
+
+        def multiply_pair(j, carry, first=first, count=count, slot=slot, block=block):
+            weight = gu[j, slot:slot + count].reshape(count * half, gu.shape[3])
+            term = jnp.dot(block, weight, preferred_element_type=F32)
+            acc[j] = term if first == 0 else acc[j] + term
+            return carry
+
+        lax.fori_loop(0, 2, multiply_pair, 0)
+        for i in range(loaded, min(loaded + count, slabs)):
+            start_pair(i)
+        loaded = min(loaded + count, slabs)
+
     sq_copy(NZ + 1).wait()
     total_row = jnp.broadcast_to((sq[NZ + 2] + sq[NZ + 3])[0:1], (rows, HD))
     total = jnp.sum(jnp.where(eye, total_row, 0.0), axis=1, keepdims=True)
@@ -361,84 +377,67 @@
     span = prod.shape[2]
     seg = zf.shape[3]
     hrows = rows // NH
-    xrows = hrows // NX
 
     def multiply(b):
-        def chunk(j, carry):
-            c = b * per + j
-            wd_copy(c).wait()
-            term = jnp.dot(hidden[...], wd[lax.rem(c, WD_SLOTS)], preferred_element_type=F32)
-            term = term + jnp.where(c == own, 1.0, 0.0) * mixed[...]
-            prod[b, :, pl.ds(pl.multiple_of(j * half, half), half)] = term
-
-            @pl.when(c + WD_SLOTS < slabs)
-            def _():
-                wd_copy(c + WD_SLOTS).start()
-
-            return carry
-
-        lax.fori_loop(0, per, chunk, 0)
+        wd_copy(b).wait()
+        prod[b] = jnp.dot(hidden[...], wd[b % WD_SLOTS], preferred_element_type=F32)
+        if b + WD_SLOTS < batches:
+            wd_copy(b + WD_SLOTS).start()
+
+        @pl.when(own // per == b)
+        def _():
+            cols = pl.ds(pl.multiple_of(lax.rem(own, per) * half, half), half)
+            prod[b, :, cols] += mixed[...]
 
     def h_copy(b):
         src = prod.at[b, pl.ds(pl.multiple_of(other_h * hrows, hrows), hrows), :]
         return remote(src, hrecv.at[b], h_send.at[b], h_recv.at[b], to_h)
 
-    def x_copy(b):
-        return remote(xsend.at[b], xrecv.at[b], x_send.at[b], x_recv.at[b], to_x)
-
-    def z_copy(b, t):
-        sem = b * (NZ - 1) + t - 1
-        return remote(zsend.at[b, z_at(t)], zrecv.at[b, t - 1], z_send.at[sem], z_recv.at[sem], to_z(t))
-
-    def stage_x(b):
+    def z_copy(b, p):
+        zi, xi = chip(p)
+        sem = b * (NZ * NX - 1) + p - 1
+        src = zsend.at[b, xi * NZ + zi]
+        return remote(src, zrecv.at[b, p - 1], z_send.at[sem], z_recv.at[sem], {"ffn": zi, "side": xi})
+
+    def stage_z(b):
         h_copy(b).wait()
         s1[b] = prod[b, pl.ds(pl.multiple_of(h * hrows, hrows), hrows), :] + hrecv[b]
-        there = s1[b, pl.ds(pl.multiple_of(other_x * xrows, xrows), xrows), :]
-        xsend[b] = jnp.concatenate([there[:, :span // 2], there[:, span // 2:]], axis=0).astype(BF16)
-        x_copy(b).start()
-
-    def stage_z(b):
-        x_copy(b).wait()
-        here = s1[b, pl.ds(pl.multiple_of(x * xrows, xrows), xrows), :]
-        came = xrecv[b].astype(F32)
-        s2[b] = here + jnp.concatenate([came[:xrows], came[xrows:]], axis=1)
-        for q in range(NZ):
+        for q in range(NZ * NX):
             for m in range(span // seg):
-                zf[b, q, m * each:(m + 1) * each, :] = s2[b, q * each:(q + 1) * each, m * seg:(m + 1) * seg]
+                zf[b, q, m * each:(m + 1) * each, :] = s1[b, q * each:(q + 1) * each, m * seg:(m + 1) * seg]
         zsend[b] = zf[b].astype(BF16)
-        for t in range(1, NZ):
-            z_copy(b, t).start()
+        for p in (7, 6, 5, 4, 3, 2, 1):
+            z_copy(b, p).start()
 
     def stage_out(b):
-        for t in range(1, NZ):
-            z_copy(b, t).wait()
-        total = zf[b, z]
-        for t in range(1, NZ):
-            total = total + zrecv[b, t - 1].astype(F32)
+        total = zf[b, x * NZ + z]
+        for p in range(1, NZ * NX):
+            z_copy(b, p).wait()
+            total = total + zrecv[b, p - 1].astype(F32)
         facc[b] = total
         for m in range(span // seg):
             at = b * span + m * seg
             out_ref[:, at:at + seg] = facc[b, m * each:(m + 1) * each, :].astype(BF16)
 
-    for step in range(batches + 3):
+    for step in range(batches + 1):
         if step < batches:
             multiply(step)
             h_copy(step).start()
-        if 0 <= step - 1 < batches:
-            stage_x(step - 1)
-        if 0 <= step - 2 < batches:
-            stage_z(step - 2)
-        if 0 <= step - 3 < batches:
-            stage_out(step - 3)
+        if step >= 1:
+            stage_z(step - 1)
+    for b in range(batches):
+        stage_out(b)
 
     for t in range(1, NZ):
         nrm_copy(own, t - 1, to_z(t)).wait_send()
     nrm_copy(own, NZ - 1, to_x).wait_send()
     nrm_copy(own, NZ, to_h).wait_send()
-    for i in range(1, NZ):
-        nrm_copy(own, NZ + i, to_x).wait_send()
-    for i in range(1, NZ * NX):
-        nrm_copy(own, 2 * NZ - 1 + i, to_h).wait_send()
+    nrm_copy(own, NZ + 1, to_h).wait_send()
+    for i in range(3, 6):
+        nrm_copy(own, NZ - 1 + i, to_x).wait_send()
+        nrm_copy(own, 2 * NZ - 2 + i, to_h).wait_send()
+    for i in range(7, 10):
+        nrm_copy(own, 2 * NZ - 3 + i, to_h).wait_send()
 
 
 def fused(
@@ -467,9 +466,8 @@
         in_specs=[vmem] * 7 + [hbm] * 4,
         out_specs=vmem,
         scratch_shapes=[
-            V((NH, out_weight.shape[0], half), BF16),
-            V((2 * GU_PAIRS, half, ff), BF16),
-            V((WD_SLOTS, ff, half), BF16),
+            V((2, PAIRS, half, ff), BF16),
+            V((WD_SLOTS, ff, span), BF16),
             V((group * cap, HD), F32),
             V((group * rows, NZ * NX * group * cap), BF16),
             V((NZ * NX, kv, group * cap, HD), BF16),
@@ -484,30 +482,25 @@
             V((batches, rows, span), F32),
             V((batches, rows // NH, span), F32),
             V((batches, rows // NH, span), F32),
-            V((batches, 16, span // 2), BF16),
-            V((batches, 16, span // 2), BF16),
-            V((batches, 8, span), F32),
-            V((batches, NZ, 16, seg), F32),
-            V((batches, NZ, 16, seg), BF16),
-            V((batches, NZ - 1, 16, seg), BF16),
+            V((batches, NZ * NX, 16, seg), F32),
+            V((batches, NZ * NX, 16, seg), BF16),
+            V((batches, NZ * NX - 1, 16, seg), BF16),
             V((batches, 16, seg), F32),
-            dma((NH,)),
-            dma((2 * GU_PAIRS,)),
+            dma((2 * WO_PAIRS,)),
+            dma((2, PAIRS)),
             dma((WD_SLOTS,)),
             dma((2 * NZ,)),
             dma((NZ * NX,)),
             dma(()),
             dma(()),
-            dma((2 * NZ + NZ * NX,)),
+            dma((4 * NZ - 1,)),
             dma((slabs,)),
             dma((NZ + 1,)),
             dma((NZ + 1,)),
             dma((batches,)),
             dma((batches,)),
-            dma((batches,)),
-            dma((batches,)),
-            dma((batches * (NZ - 1),)),
-            dma((batches * (NZ - 1),)),
+            dma((batches * (NZ * NX - 1),)),
+            dma((batches * (NZ * NX - 1),)),
         ],
         cost_estimate=pl.CostEstimate(
             flops=2 * rows * weights, bytes_accessed=2 * weights, transcendentals=rows * ff

time: 54.8 us -> 46.3 us (0.84)
  Pallas kernels: 53.2 us -> 44.7 us
    pallas_call x1, Pallas kernels: 53.2 us -> 44.7 us  [fused(): pl.pallas_call(fused_kernel, out_shape=jax.ShapeDtypeStruct((each, slabs...]
where the time goes in v2:
time: 46.3 us; the launch traced here: 46.1 us
  Pallas kernels  44.7 us (97%)
  local copies, waits for them, and re-layouts  1.4 us (3%)
    pallas_call x1, Pallas kernels, fused(): pl.pallas_call(fused_kernel, out_shape=jax.ShapeDtypeStruct((each, slabs...  44.7 us
    unnamed x1, local copies, waits for them, and re-layouts  1.4 us

profile of v2, /device:TPU:0, one launch (start us, length us, event | category | flops | bytes accessed | tf_op | source)
XLA Modules:
  0.0 46.1 jit_solution(10421617208524408608)
XLA Ops:
  0.0 44.7 %shard_map.109 = bf16[2,8192]{1,0:T(2,128)(2,1)} custom-call(s32[1,32]{1,0:T(1,128)} %bitcast.4, s32[1,32]{1,0:T(1,128)} %bitcast.5, f32[1,8192]{1,0:T(1,128)} %bitcast.3, bf16[32,1024]{1,0:T(8,128)(2,1)} %resid_ref.1, bf16[5,4096]{1,0:T(8,128)(2,1)} %q_ref.1, bf16[5,128,256]{2,1,0:T(8,128)(2,1)} %k_ref.1, bf16[5,128,256]{2,1,0:T(8,128)(2,1)} %v_ref.1, ...), custom_call_target="tpu_custom_call" | custom-call | flops 2885681152 | bytes 90177536 | tf_op jit(solution)/shard_map/pallas_call | solution.py:463
  44.7 1.4 %copy.13 = bf16[2,8192]{1,0:T(2,128)(2,1)} copy(bf16[2,8192]{1,0:T(2,128)(2,1)} %shard_map.109) | data formatting | bytes 65536

commit v3 on v2

--- a/solution.py
+++ b/solution.py
@@ -91,10 +91,10 @@
 WD_SLOTS = 3
 WO_PAIRS = 4
 EARLY = 2
-RUNS = ((0,), (1, 2), (3, 4, 5), (6,), (7, 8, 9, 10), (11, 12, 13), (14, 15))
+RUNS = ((0,), (1,), (2,), (3, 4, 5, 6), (7, 8, 9), (10, 11, 12), (13, 14, 15))
 STEPS = (
-    (0, 0, 0), (0, 0, 1), (0, 1, 0), (1, 0, 0), (2, 0, 0), (3, 0, 0), (0, 1, 1), (1, 1, 0),
-    (2, 1, 0), (3, 1, 0), (1, 0, 1), (2, 0, 1), (3, 0, 1), (1, 1, 1), (2, 1, 1), (3, 1, 1),
+    (0, 0, 0), (0, 0, 1), (0, 1, 0), (0, 1, 1), (1, 0, 0), (2, 0, 0), (3, 0, 0), (1, 0, 1),
+    (2, 0, 1), (3, 0, 1), (1, 1, 0), (2, 1, 0), (3, 1, 0), (1, 1, 1), (2, 1, 1), (3, 1, 1),
 )
 F32 = jnp.float32
 BF16 = jnp.bfloat16
@@ -214,15 +214,20 @@
         spread = jnp.concatenate(
             [jnp.where(of_slot == c, probs, 0.0) for c in range(cap)], axis=1
         ).astype(BF16)
-        att[dev, k] = jnp.dot(spread, values, preferred_element_type=F32).astype(BF16)
+        att[dev, :, k * HD:(k + 1) * HD] = jnp.dot(
+            spread, values, preferred_element_type=F32
+        ).astype(BF16)
 
     pl.semaphore_wait(barrier, NZ * NX)
 
-    def att_copy(d, sem, where):
-        return remote(att.at[d], att.at[d], att_send.at[sem], att_recv.at[d], where)
-
-    att_out = [att_copy(dev, t - 1, to_z(t)) for t in range(1, NZ)]
-    att_out.append(att_copy(dev, NZ - 1, to_x))
+    def att_copy(d, sem, where, k):
+        part = att.at[d, :, pl.ds(k * HD, HD)]
+        return remote(part, part, att_send.at[k, sem], att_recv.at[k, d], where)
+
+    att_out = []
+    for k in range(kv):
+        att_out.append(att_copy(dev, NZ - 1, to_x, k))
+        att_out += [att_copy(dev, t - 1, to_z(t), k) for t in range(1, NZ)]
     for copy in att_out:
         copy.start()
 
@@ -247,21 +252,23 @@
     resid_half = resid_ref[:, pl.ds(pl.multiple_of(h * half, half), half)]
     mixed[...] = jnp.dot(row_pick.astype(F32).astype(BF16), resid_half, preferred_element_type=F32)
 
-    for t in range(1, NZ):
-        d = z_at(t) * NX + x
-        att_copy(d, 0, to_x).wait_recv()
-        fwd = att_copy(d, NZ - 1 + t, to_x)
-        fwd.start()
-        att_out.append(fwd)
-    for t in range(NZ):
-        d = z_at(t) * NX + other_x
-        att_copy(d, 0, to_x).wait_recv()
     for k in range(kv):
-        blocks = att[:, k].reshape(NZ * NX * group * cap, HD)
-        moved = jnp.dot(place[...], blocks, preferred_element_type=F32).astype(BF16)
+        for t in range(1, NZ):
+            d = z_at(t) * NX + x
+            att_copy(d, 0, to_x, k).wait_recv()
+            fwd = att_copy(d, NZ - 1 + t, to_x, k)
+            fwd.start()
+            att_out.append(fwd)
+    for k in range(kv):
+        for t in range(NZ):
+            d = z_at(t) * NX + other_x
+            att_copy(d, 0, to_x, k).wait_recv()
+    blocks = att[...].reshape(NZ * NX * group * cap, kv * HD)
+    moved = jnp.dot(place[...], blocks, preferred_element_type=F32).astype(BF16)
+    for k in range(kv):
         for g in range(group):
             at = (k * group + g) * HD
-            lhs[:, at:at + HD] = moved[g * rows:(g + 1) * rows, :]
+            lhs[:, at:at + HD] = moved[g * rows:(g + 1) * rows, k * HD:(k + 1) * HD]
     for copy in att_out:
         copy.wait_send()
 
@@ -295,10 +302,10 @@
     def nrm_copy(s, sem, where):
         return remote(nrm.at[s], nrm.at[s], nrm_send.at[sem], nrm_recv.at[s], where)
 
+    nrm_copy(own, NZ, to_h).start()
+    nrm_copy(own, NZ - 1, to_x).start()
     for t in range(1, NZ):
         nrm_copy(own, t - 1, to_z(t)).start()
-    nrm_copy(own, NZ - 1, to_x).start()
-    nrm_copy(own, NZ, to_h).start()
 
     squares = jnp.sum(mix * mix, axis=1, keepdims=True)
     eye = iota((rows, HD), 0) == iota((rows, HD), 1)
@@ -322,28 +329,28 @@
     loaded = PAIRS
     for run in RUNS:
         first, count = run[0], len(run)
-        if first == 1:
+        if first == 2:
             arrived(2)
             pass_on(2, NZ + 1, to_h)
-            arrived(1)
         elif first == 3:
+            for i in run[1:]:
+                arrived(i)
+                pass_on(i, NZ - 2 + i, to_x)
+                pass_on(i, 2 * NZ - 3 + i, to_h)
+            arrived(3)
+        elif first == 10:
             for i in run:
                 arrived(i)
-                pass_on(i, NZ - 1 + i, to_x)
-                pass_on(i, 2 * NZ - 2 + i, to_h)
-        elif first == 7:
-            for i in run[:-1]:
+                pass_on(i, NZ - 2 + i, to_h)
+        elif first > 0:
+            for i in run:
                 arrived(i)
-                pass_on(i, 2 * NZ - 3 + i, to_h)
-            arrived(run[-1])
+        if first == 7:
             for t in range(1, NZ):
                 sq_copy(t).wait()
             sq[NZ] = sq[0] + sq[1] + sq[2] + sq[3]
             sq_copy(NZ).start()
-        elif first > 0:
-            for i in run:
-                arrived(i)
-        if first == 11:
+        elif first == 13:
             sq_copy(NZ).wait()
             sq[NZ + 2] = sq[NZ] + sq[NZ + 1]
             sq_copy(NZ + 1).start()
@@ -433,11 +440,11 @@
     nrm_copy(own, NZ - 1, to_x).wait_send()
     nrm_copy(own, NZ, to_h).wait_send()
     nrm_copy(own, NZ + 1, to_h).wait_send()
-    for i in range(3, 6):
-        nrm_copy(own, NZ - 1 + i, to_x).wait_send()
-        nrm_copy(own, 2 * NZ - 2 + i, to_h).wait_send()
-    for i in range(7, 10):
+    for i in range(4, 7):
+        nrm_copy(own, NZ - 2 + i, to_x).wait_send()
         nrm_copy(own, 2 * NZ - 3 + i, to_h).wait_send()
+    for i in range(10, 13):
+        nrm_copy(own, NZ - 2 + i, to_h).wait_send()
 
 
 def fused(
@@ -470,7 +477,7 @@
             V((WD_SLOTS, ff, span), BF16),
             V((group * cap, HD), F32),
             V((group * rows, NZ * NX * group * cap), BF16),
-            V((NZ * NX, kv, group * cap, HD), BF16),
+            V((NZ * NX, group * cap, kv * HD), BF16),
             V((rows, out_weight.shape[0]), BF16),
             V((rows, half), F32),
             V((rows, half), F32),
@@ -489,8 +496,8 @@
             dma((2 * WO_PAIRS,)),
             dma((2, PAIRS)),
             dma((WD_SLOTS,)),
-            dma((2 * NZ,)),
-            dma((NZ * NX,)),
+            dma((kv, 2 * NZ)),
+            dma((kv, NZ * NX)),
             dma(()),
             dma(()),
             dma((4 * NZ - 1,)),

time: 46.3 us -> 46.4 us (level)
  no operation moved by 1% of the time
where the time goes in v3:
time: 46.4 us; the launch traced here: 46.2 us
  Pallas kernels  44.8 us (97%)
  local copies, waits for them, and re-layouts  1.4 us (3%)
    pallas_call x1, Pallas kernels, fused(): pl.pallas_call(fused_kernel, out_shape=jax.ShapeDtypeStruct((each, slabs...  44.8 us
    unnamed x1, local copies, waits for them, and re-layouts  1.4 us

profile of v3, /device:TPU:0, one launch (start us, length us, event | category | flops | bytes accessed | tf_op | source)
XLA Modules:
  0.0 46.2 jit_solution(7200752126030753539)
XLA Ops:
  0.0 44.8 %shard_map.109 = bf16[2,8192]{1,0:T(2,128)(2,1)} custom-call(s32[1,32]{1,0:T(1,128)} %bitcast.4, s32[1,32]{1,0:T(1,128)} %bitcast.5, f32[1,8192]{1,0:T(1,128)} %bitcast.3, bf16[32,1024]{1,0:T(8,128)(2,1)} %resid_ref.1, bf16[5,4096]{1,0:T(8,128)(2,1)} %q_ref.1, bf16[5,128,256]{2,1,0:T(8,128)(2,1)} %k_ref.1, bf16[5,128,256]{2,1,0:T(8,128)(2,1)} %v_ref.1, ...), custom_call_target="tpu_custom_call" | custom-call | flops 2885681152 | bytes 90177536 | tf_op jit(solution)/shard_map/pallas_call | solution.py:470
  44.8 1.4 %copy.13 = bf16[2,8192]{1,0:T(2,128)(2,1)} copy(bf16[2,8192]{1,0:T(2,128)(2,1)} %shard_map.109) | data formatting | bytes 65536
